TPU v7x, 32 devices: a whole 2x2x4 slice. The times are simulated.
32 devices in a mesh: pair: 8 (over z, x), vgrp: 4 (over y, core).
Axes of the slice: x: 2, y: 2, z: 4, core: 2. Of those that a mesh axis runs over, the one named last changes fastest.
Arguments:
- amplitudes: bfloat16 [16, 768, 768], P('pair'), may hold values from -6 to 6
- cholesky_vectors: bfloat16 [4, 8, 768, 768], P('vgrp', 'pair'), may hold values from -0.21875 to 0.21875
- owner_order: int32 [4, 4], replicated, may hold values from 0 to 7, as said below
Outputs:
- residual: float32 [16, 768, 768], P('pair', 'vgrp')
Inputs may be any that keep to these rules, and one draw needn't show every extreme that they name: `owner_order`: within one row the 4 entries are distinct; in every draw some row names both 0 and 7.
All inputs are finite; a program needn't handle non-finite values.
Results may differ from a plain program's by a relative error of at most 0.0029.
Values may be sent and summed in bfloat16 or wider, within the bound.
A program may use at most 64 MiB of HBM per device.

v0:
```python
import jax
import jax.numpy as jnp
from jax import lax
from jax.sharding import PartitionSpec as P


def spread(block, axis, source):
    block = jnp.where(lax.axis_index(axis) == source, block, jnp.zeros_like(block))
    return lax.psum(block, axis)


def on_device(amplitudes, cholesky_vectors, owner_order):
    vgrp_index = lax.axis_index("vgrp")
    owned_slots = lax.dynamic_index_in_dim(owner_order, vgrp_index, 0, keepdims=False)
    own_vector = cholesky_vectors[0, 0]
    slot_count = owned_slots.shape[0]
    accumulated = jnp.zeros(amplitudes.shape, jnp.float32)
    for slot in range(slot_count):
        vector = spread(own_vector, "pair", owned_slots[slot])
        half_product = jnp.einsum(
            "ac,pcd->pad", vector, amplitudes, preferred_element_type=jnp.float32
        ).astype(jnp.bfloat16)
        accumulated = accumulated + jnp.einsum(
            "pad,bd->pab", half_product, vector, preferred_element_type=jnp.float32
        )
    return lax.psum_scatter(accumulated, "vgrp", scatter_dimension=1, tiled=True)


def solution(mesh):
    placed = (P("pair", None, None), P("vgrp", "pair", None, None), P())
    return jax.shard_map(
        on_device, mesh=mesh, in_specs=placed, out_specs=P("pair", "vgrp", None), check_vma=False
    )
```

profile of v0, /device:TPU:0, one launch (start us, length us, event | category | flops | bytes accessed | tf_op | source)
XLA Modules:
  0.0 271.8 jit_solution(2178326192421937889)
XLA Ops:
  6.5 0.0 copy-start
  6.5 0.0 all-reduce.3.cloned.1.call-start
  6.5 0.8 constant_dynamic-slice_fusion
  7.4 0.7 fusion.42
  10.6 3.6 %select_bitcast_fusion.3 = (bf16[768,768]{1,0:T(8,128)(2,1)}, bf16[768,768]{1,0:T(8,128)(2,1)}, bf16[768,768]{1,0:T(8,128)(2,1)}, bf16[768,768]{1,0:T(8,128)(2,1)}) fusion(bf16[1,1,768,768]{3,2,1,0:T(8,128)(2,1)} %param.4, pred[]{:T(512)S(6)} %eq.12, pred[]{:T(512)S(6)} %eq.13, pred[]{:T(512)S(6)} %eq.15, pred[]{:T(512)S(6)} %eq.14), kind=kLoop, calls=%fused_computation.28 | loop fusion | flops 2359296 | bytes 5898244 | tf_op jit(solution)/shard_map/jit(_where)/select_n | solution.py:8
  14.1 0.0 all-reduce.3.cloned.1.call-update
  14.1 0.0 reduce-scatter.2.cloned.1.call-start
  14.2 173.5 %all-reduce.3.cloned.1.call-done = (bf16[768,768]{1,0:T(8,128)(2,1)}, bf16[768,768]{1,0:T(8,128)(2,1)}, bf16[768,768]{1,0:T(8,128)(2,1)}, bf16[768,768]{1,0:T(8,128)(2,1)}) async-done(((bf16[768,768]{1,0:T(8,128)(2,1)}, bf16[768,768]{1,0:T(8,128)(2,1)}, bf16[768,768]{1,0:T(8,128)(2,1)}, bf16[768,768]{1,0:T(8,128)(2,1)}), (bf16[768,768]{1,0:T(8,128)(2,1)}, bf16[768,768]{1,0:T(8,128)(2,1)}, ...) | async-done | bytes 4718608 | tf_op jit(solution)/shard_map/psum | solution.py:9
  187.7 0.0 copy-done
  187.7 0.0 copy-start.2
  187.7 7.7 %fusion = f32[2,768,768]{2,1,0:T(8,128)} fusion(bf16[768,768]{1,0:T(8,128)(2,1)} %get-tuple-element.5, bf16[2,768,768]{2,1,0:T(8,128)(2,1)S(1)} %copy-done), kind=kOutput, calls=%fused_computation.1 | convolution fusion | flops 3625058304 | bytes 8257536 | tf_op jit(solution)/shard_map/pad,bd->pab/dot_general | solution.py:23
  195.5 0.0 copy-done.2
  195.5 6.0 %fusion.2 = f32[2,768,768]{2,1,0:T(8,128)} fusion(bf16[768,768]{1,0:T(8,128)(2,1)S(1)} %copy-done.2, bf16[2,768,768]{2,1,0:T(8,128)(2,1)S(1)} %copy-done), kind=kOutput, calls=%fused_computation.3 | convolution fusion | flops 3625058304 | bytes 8257536 | tf_op jit(solution)/shard_map/pad,bd->pab/dot_general | solution.py:23
  201.5 0.0 copy-start.1
  201.5 7.8 %fusion.4 = f32[2,768,768]{2,1,0:T(8,128)} fusion(bf16[768,768]{1,0:T(8,128)(2,1)} %get-tuple-element.7, bf16[2,768,768]{2,1,0:T(8,128)(2,1)S(1)} %copy-done), kind=kOutput, calls=%fused_computation.5 | convolution fusion | flops 3625058304 | bytes 8257536 | tf_op jit(solution)/shard_map/pad,bd->pab/dot_general | solution.py:23
  209.3 0.0 copy-done.1
  209.3 8.8 %add_add_fusion = f32[2,768,768]{2,1,0:T(8,128)} fusion(f32[2,768,768]{2,1,0:T(8,128)} %fusion, f32[2,768,768]{2,1,0:T(8,128)} %fusion.2, f32[2,768,768]{2,1,0:T(8,128)} %fusion.4, bf16[768,768]{1,0:T(8,128)(2,1)S(1)} %copy-done.1, bf16[2,768,768]{2,1,0:T(8,128)(2,1)S(1)} %copy-done), kind=kOutput, calls=%fused_computation | convolution fusion | flops 3628597248 | bytes 22413312 | tf_op jit(solution)/shard_map/pad,bd->pab/dot_general | solution.py:23
  218.0 0.0 reduce-scatter.2.cloned.1.call-update
  218.1 46.9 %reduce-scatter.2.cloned.1.call-done = f32[2,192,768]{2,1,0:T(8,128)} async-done(((f32[2,768,768]{2,1,0:T(8,128)}), f32[2,192,768]{2,1,0:T(8,128)}) %reduce-scatter.2.cloned.1.call-update) | async-done | bytes 1179664 | tf_op jit(solution)/shard_map/reduce_scatter | solution.py:26
Async XLA Ops:
  6.5 181.2 %copy-start = (bf16[2,768,768]{2,1,0:T(8,128)(2,1)S(1)}, bf16[2,768,768]{2,1,0:T(8,128)(2,1)}, u32[]{:S(2)}) copy-start(bf16[2,768,768]{2,1,0:T(8,128)(2,1)} %param.3) | copy-start | bytes 7077892
  6.5 181.2 %all-reduce.3.cloned.1.call-start = ((), (), s32[]{:S(2)}) async-start(), calls=%async_computation.2 | async-start | bytes 9437184 | tf_op jit(solution)/shard_map/psum | solution.py:9
  14.1 250.8 %reduce-scatter.2.cloned.1.call-start = ((), (), s32[]{:S(2)}) async-start(), calls=%async_computation.1 | async-start | bytes 5898240 | tf_op jit(solution)/shard_map/reduce_scatter | solution.py:26
  187.7 7.7 %copy-start.2 = (bf16[768,768]{1,0:T(8,128)(2,1)S(1)}, bf16[768,768]{1,0:T(8,128)(2,1)}, u32[]{:S(2)}) copy-start(bf16[768,768]{1,0:T(8,128)(2,1)} %get-tuple-element.6) | copy-start | bytes 3538948
  201.5 7.8 %copy-start.1 = (bf16[768,768]{1,0:T(8,128)(2,1)S(1)}, bf16[768,768]{1,0:T(8,128)(2,1)}, u32[]{:S(2)}) copy-start(bf16[768,768]{1,0:T(8,128)(2,1)} %get-tuple-element.8) | copy-start | bytes 3538948
Sparse Core Ops, SparseCore 0:
  14.3 173.4 all-reduce.2
  218.2 46.7 reduce-scatter.1
where the time goes:
time: 272 us
  waiting for transfers between devices  220 us (81%)
  matrix products  30.3 us (11%)
  between operations  15.9 us (6%)
  other arithmetic  3.55 us (1%)
    psum x1, waiting for transfers between devices, spread(): return lax.psum(block, axis)  174 us
    reduce_scatter x1, waiting for transfers between devices, on_device(): lax.psum_scatter(accumulated, 'vgrp', scatter_dimension=1, tiled=True)  46.9 us
    dot_general x4, matrix products, on_device(): jnp.einsum('pad,bd->pab', half_product, vector, preferred_element_type=jn...  30.3 us
  transfers between devices with their start and end apart: 2, of which 2 were waited for; matrix products, arithmetic and copies ran while one was open for 0% of the time, Pallas kernels for 0%

commit v1 on v0

v1 whole, which is shorter than its diff:
```python
import functools

import jax
import jax.numpy as jnp
from jax import lax
from jax.experimental import pallas as pl
from jax.experimental.pallas import tpu as pltpu
from jax.sharding import PartitionSpec as P

MESH = pl.DeviceIdType.MESH
CHUNKS = 4
LAG = 2
F32 = jnp.float32
BF16 = jnp.bfloat16


def kernel(
    nz, slots, owner_ref, amp_hbm, vec_ref, out_ref,
    amp, near, right_in, left_in, right_out, left_out, vectors, halves, acc,
    core_out, core_in, y_out, y_in,
    amp_sem, near_send, near_recv, rs_sem, rr_sem, ls_sem, lr_sem,
    fs_sem, fr_sem, cs_sem, cr_sem, ys_sem, yr_sem,
):
    pair = lax.axis_index("pair")
    grp = lax.axis_index("vgrp")
    z, x = pair // 2, pair % 2
    y, core = grp // 2, grp % 2
    size = vec_ref.shape[0]
    half = size // 2
    part = half // CHUNKS
    items = slots * CHUNKS
    pairs, tile = out_ref.shape[0], out_ref.shape[1]
    last = nz - 1

    x_dev = {"pair": z * 2 + (1 - x), "vgrp": grp}
    up_dev = {"pair": ((z + 1) % nz) * 2 + x, "vgrp": grp}
    down_dev = {"pair": ((z + last) % nz) * 2 + x, "vgrp": grp}
    core_dev = {"pair": pair, "vgrp": y * 2 + (1 - core)}
    y_dev = {"pair": pair, "vgrp": (1 - y) * 2 + core}

    load = pltpu.make_async_copy(amp_hbm, amp, amp_sem)
    load.start()

    barrier = pltpu.get_barrier_semaphore()
    for dev in (x_dev, up_dev, down_dev, core_dev, y_dev):
        pl.semaphore_signal(barrier, inc=1, device_id=dev, device_id_type=MESH)
    pl.semaphore_wait(barrier, 5)

    def remote(src, dst, send, recv, dev):
        return pltpu.make_async_remote_copy(
            src_ref=src, dst_ref=dst, send_sem=send, recv_sem=recv,
            device_id=dev, device_id_type=MESH,
        )

    def near_copy(c):
        rows = pl.ds(pl.multiple_of((1 - x) * half + c * part, 16), part)
        return remote(vec_ref.at[rows], near.at[c], near_send.at[c], near_recv.at[c], x_dev)

    def right_copy(i):
        return remote(right_out.at[i], right_in.at[i], rs_sem.at[i], rr_sem.at[i], up_dev)

    def left_copy(i):
        return remote(left_out.at[i], left_in.at[i], ls_sem.at[i], lr_sem.at[i], down_dev)

    def my_rows(i):
        return pl.ds(pl.multiple_of(x * half + (i % CHUNKS) * part, 16), part)

    def final_copy(i):
        view = vectors.at[i // CHUNKS, my_rows(i)]
        return remote(view, view, fs_sem.at[i], fr_sem.at[i], x_dev)

    def owner(i):
        o = owner_ref[grp, i // CHUNKS]
        return o // 2, o % 2

    def local(i):
        unused, ox = owner(i)
        return lax.select(ox == x, vec_ref[my_rows(i), :], near[i % CHUNKS])

    for c in range(CHUNKS):
        near_copy(c).start()
    acc[...] = jnp.zeros_like(acc)

    lag_r = LAG * z
    lag_l = LAG * (last - z)
    lag_f = LAG * last
    first = lag_f + CHUNKS + 1
    per_slot = 2 * pairs + 4

    def through(k, rows):
        lhs = halves[:, rows, :].reshape(pairs * tile, size)
        more = lax.dot_general(
            lhs, vectors[k], (((1,), (1,)), ((), ())), preferred_element_type=F32
        ).reshape(pairs, tile, size)
        return acc[:, rows, :] + more

    def piece(q):
        k, j = q // per_slot, q % per_slot

        @pl.when(j == 0)
        def _():
            for c in range(CHUNKS):
                final_copy(k * CHUNKS + c).wait_recv()

        @pl.when(j < 2 * pairs)
        def _():
            p = j // 2
            rows = pl.ds(pl.multiple_of((j % 2) * half, 16), half)
            halves[p, rows, :] = jnp.dot(
                vectors[k, rows, :], amp[p], preferred_element_type=F32
            ).astype(BF16)

        @pl.when(j >= 2 * pairs)
        def _():
            rows = pl.ds(pl.multiple_of((j - 2 * pairs) * tile, 16), tile)
            acc[:, rows, :] = through(k, rows)

    def step(t, carry):
        @pl.when(t < CHUNKS)
        def _():
            near_copy(t).wait_recv()

        i = t - lag_r

        @pl.when((i >= 0) & (i < items))
        def _():
            @pl.when(z > 0)
            def _():
                right_copy(i).wait_recv()

            @pl.when(z == 0)
            def _():
                right_out[i] = local(i)
                right_copy(i).start()

            @pl.when((z > 0) & (z < last))
            def _():
                oz, unused = owner(i)
                right_out[i] = lax.select(oz == z, local(i), right_in[i])
                right_copy(i).start()

        j = t - lag_l

        @pl.when((j >= 0) & (j < items))
        def _():
            @pl.when(z < last)
            def _():
                left_copy(j).wait_recv()

            @pl.when(z == last)
            def _():
                left_out[j] = local(j)
                left_copy(j).start()

            @pl.when((z > 0) & (z < last))
            def _():
                oz, unused = owner(j)
                left_out[j] = lax.select(oz == z, local(j), left_in[j])
                left_copy(j).start()

        f = t - lag_f

        @pl.when((f >= 0) & (f < items))
        def _():
            oz, unused = owner(f)
            k, rows = f // CHUNKS, my_rows(f)

            @pl.when(z == 0)
            def _():
                vectors[k, rows, :] = lax.select(oz == z, local(f), left_in[f])

            @pl.when(z == last)
            def _():
                vectors[k, rows, :] = lax.select(oz == z, local(f), right_in[f])

            @pl.when((z > 0) & (z < last))
            def _():
                came = lax.select(oz < z, right_in[f], left_in[f])
                vectors[k, rows, :] = lax.select(oz == z, local(f), came)

            final_copy(f).start()

        @pl.when(t == first)
        def _():
            load.wait()

        q = (t - first) * 2
        for n in range(2):
            @pl.when((q + n >= 0) & (q + n < slots * per_slot - 4))
            def _():
                piece(q + n)

        return carry

    lax.fori_loop(0, first + slots * per_slot // 2, step, 0)

    k = slots - 1

    def rows_of(yy, cc):
        return pl.ds(pl.multiple_of((yy * 2 + cc) * tile, 16), tile)

    def core_copy(n):
        return remote(core_out.at[n], core_in.at[n], cs_sem.at[n], cr_sem.at[n], core_dev)

    def y_copy(p):
        return remote(y_out.at[p], y_in.at[p], ys_sem.at[p], yr_sem.at[p], y_dev)

    core_out[0] = through(k, rows_of(1 - y, 1 - core)).astype(BF16)
    core_copy(0).start()
    core_out[1] = through(k, rows_of(y, 1 - core)).astype(BF16)
    core_copy(1).start()
    rows = rows_of(1 - y, core)
    acc[:, rows, :] = through(k, rows)
    core_copy(0).wait_recv()
    for p in range(pairs):
        y_out[p] = (acc[p, rows, :] + core_in[0, p].astype(F32)).astype(BF16)
        y_copy(p).start()
    rows = rows_of(y, core)
    acc[:, rows, :] = through(k, rows)
    core_copy(1).wait_recv()
    for p in range(pairs):
        y_copy(p).wait_recv()
        out_ref[p] = acc[p, rows, :] + core_in[1, p].astype(F32) + y_in[p].astype(F32)

    for c in range(CHUNKS):
        near_copy(c).wait_send()

    def drain(i, carry):
        @pl.when(z < last)
        def _():
            right_copy(i).wait_send()

        @pl.when(z > 0)
        def _():
            left_copy(i).wait_send()

        final_copy(i).wait_send()
        return carry

    lax.fori_loop(0, items, drain, 0)
    for n in range(2):
        core_copy(n).wait_send()
    for p in range(pairs):
        y_copy(p).wait_send()


def on_device(pair_size, amplitudes, cholesky_vectors, owner_order):
    pairs, size, unused = amplitudes.shape
    slots = owner_order.shape[1]
    half = size // 2
    part = half // CHUNKS
    items = slots * CHUNKS
    tile = size // 4
    dma = pltpu.SemaphoreType.DMA
    vmem = pltpu.VMEM
    return pl.pallas_call(
        functools.partial(kernel, pair_size // 2, slots),
        out_shape=jax.ShapeDtypeStruct((pairs, tile, size), F32),
        in_specs=[
            pl.BlockSpec(memory_space=pltpu.SMEM),
            pl.BlockSpec(memory_space=pl.ANY),
            pl.BlockSpec(memory_space=pltpu.VMEM),
        ],
        out_specs=pl.BlockSpec(memory_space=pltpu.VMEM),
        scratch_shapes=[
            vmem((pairs, size, size), BF16),
            vmem((CHUNKS, part, size), BF16),
            vmem((items, part, size), BF16),
            vmem((items, part, size), BF16),
            vmem((items, part, size), BF16),
            vmem((items, part, size), BF16),
            vmem((slots, size, size), BF16),
            vmem((pairs, size, size), BF16),
            vmem((pairs, size, size), F32),
            vmem((2, pairs, tile, size), BF16),
            vmem((2, pairs, tile, size), BF16),
            vmem((pairs, tile, size), BF16),
            vmem((pairs, tile, size), BF16),
            dma,
            dma((CHUNKS,)), dma((CHUNKS,)),
            dma((items,)), dma((items,)),
            dma((items,)), dma((items,)),
            dma((items,)), dma((items,)),
            dma((2,)), dma((2,)),
            dma((pairs,)), dma((pairs,)),
        ],
        compiler_params=pltpu.CompilerParams(
            collective_id=0, has_side_effects=True, vmem_limit_bytes=52 * 2 ** 20
        ),
        cost_estimate=pl.CostEstimate(
            flops=4 * pairs * slots * size ** 3, bytes_accessed=8 * pairs * size ** 2,
            transcendentals=0,
        ),
    )(owner_order, amplitudes, cholesky_vectors[0, 0])


def solution(mesh):
    placed = (P("pair", None, None), P("vgrp", "pair", None, None), P())
    return jax.shard_map(
        functools.partial(on_device, mesh.shape["pair"]), mesh=mesh, in_specs=placed,
        out_specs=P("pair", "vgrp", None), check_vma=False,
    )
```

time: 272 us -> 104 us (0.38)
  waiting for transfers between devices: 220 us -> 0 us
  Pallas kernels: 0 us -> 102 us
  matrix products: 30.3 us -> 0 us
  between operations: 15.9 us -> 0.01 us
  other arithmetic: 3.55 us -> 0 us
    psum x1 -> x0, waiting for transfers between devices: 174 us -> none  [spread(): return lax.psum(block, axis)]
    pallas_call x0 -> x1, Pallas kernels: none -> 102 us  [on_device(): pl.pallas_call(functools.partial(kernel, pair_size // 2, slots), out_shap...]
    reduce_scatter x1 -> x0, waiting for transfers between devices: 46.9 us -> none  [on_device(): lax.psum_scatter(accumulated, 'vgrp', scatter_dimension=1, tiled=True)]
    dot_general x4 -> x0, matrix products: 30.3 us -> none  [on_device(): jnp.einsum('pad,bd->pab', half_product, vector, preferred_element_type=jn...]
    select_n x1 -> x0, other arithmetic: 3.55 us -> none  [spread(): jnp.where(lax.axis_index(axis) == source, block, jnp.zeros_like(block))]
  transfers between devices with their start and end apart: 2 -> 0, of which waited for: 2 -> 0; matrix products, arithmetic and copies ran while one was open for 0% -> 0% of each run, Pallas kernels for 0% -> 0%
where the time goes in v1:
time: 104 us
  Pallas kernels  102 us (98%)
  local copies, waits for them, and re-layouts  1.7 us (2%)
    pallas_call x1, Pallas kernels, on_device(): pl.pallas_call(functools.partial(kernel, pair_size // 2, slots), out_shap...  102 us

profile of v1, /device:TPU:0, one launch (start us, length us, event | category | flops | bytes accessed | tf_op | source)
XLA Modules:
  0.0 104.2 jit_solution(9037504149946184571)
XLA Ops:
  0.0 0.0 copy-start
  0.0 0.7 copy-done
  0.7 102.5 %shard_map.37 = f32[2,192,768]{2,1,0:T(8,128)S(1)} custom-call(s32[4,4]{1,0:T(4,128)S(1)} %copy-done, bf16[2,768,768]{2,1,0:T(8,128)(2,1)} %amp_hbm.1, bf16[768,768]{1,0:T(8,128)(2,1)} %bitcast.1), custom_call_target="tpu_custom_call" | custom-call | flops 14495514624 | bytes 9437184 | tf_op jit(solution)/shard_map/pallas_call | solution.py:256
  103.2 1.0 copy.5
Async XLA Ops:
  0.0 0.7 copy-start

commit v2 on v1

v2 whole, which is shorter than its diff:
```python
import functools

import jax
import jax.numpy as jnp
from jax import lax
from jax.experimental import pallas as pl
from jax.experimental.pallas import tpu as pltpu
from jax.sharding import PartitionSpec as P

MESH = pl.DeviceIdType.MESH
COLS = 128
LAG = 2
F32 = jnp.float32
BF16 = jnp.bfloat16


def kernel(
    nz, slots, owner_ref, amp_hbm, vec_ref, out_ref,
    amp, near, right_in, left_in, right_out, left_out, vectors, turned, halves, acc,
    core_out, core_in, keep, y_out, y_in, rest_out, rest_in,
    amp_sem, near_send, near_recv, rs_sem, rr_sem, ls_sem, lr_sem,
    fs_sem, fr_sem, cs_sem, cr_sem, ys_sem, yr_sem, es_sem, er_sem,
):
    pair = lax.axis_index("pair")
    grp = lax.axis_index("vgrp")
    z, x = pair // 2, pair % 2
    y, core = grp // 2, grp % 2
    size = vec_ref.shape[0]
    half = size // 2
    part = COLS // 2
    chunks = size // COLS
    early = chunks // 2
    items = slots * chunks
    pairs, tile = out_ref.shape[0], out_ref.shape[1]
    last = nz - 1

    x_dev = {"pair": z * 2 + (1 - x), "vgrp": grp}
    up_dev = {"pair": ((z + 1) % nz) * 2 + x, "vgrp": grp}
    down_dev = {"pair": ((z + last) % nz) * 2 + x, "vgrp": grp}
    core_dev = {"pair": pair, "vgrp": y * 2 + (1 - core)}
    y_dev = {"pair": pair, "vgrp": (1 - y) * 2 + core}

    load = pltpu.make_async_copy(amp_hbm, amp, amp_sem)
    load.start()

    barrier = pltpu.get_barrier_semaphore()
    for dev in (x_dev, up_dev, down_dev, core_dev, y_dev):
        pl.semaphore_signal(barrier, inc=1, device_id=dev, device_id_type=MESH)
    pl.semaphore_wait(barrier, 5)

    def remote(src, dst, send, recv, dev):
        return pltpu.make_async_remote_copy(
            src_ref=src, dst_ref=dst, send_sem=send, recv_sem=recv,
            device_id=dev, device_id_type=MESH,
        )

    def start_of(c):
        there = (c // early) * y + (1 - c // early) * (1 - y)
        return there * half + (c % early) * COLS

    def rows_at(c, xx):
        return pl.ds(pl.multiple_of(start_of(c) + xx * part, 16), part)

    def block_at(c):
        return pl.ds(pl.multiple_of(start_of(c), COLS), COLS)

    def near_copy(c):
        return remote(
            vec_ref.at[rows_at(c, 1 - x)], near.at[c], near_send.at[c], near_recv.at[c], x_dev
        )

    def right_copy(i):
        return remote(right_out.at[i], right_in.at[i], rs_sem.at[i], rr_sem.at[i], up_dev)

    def left_copy(i):
        return remote(left_out.at[i], left_in.at[i], ls_sem.at[i], lr_sem.at[i], down_dev)

    def my_rows(i):
        return rows_at(i // slots, x)

    def final_copy(i):
        view = vectors.at[i % slots, my_rows(i)]
        return remote(view, view, fs_sem.at[i], fr_sem.at[i], x_dev)

    def owner(i):
        o = owner_ref[grp, i % slots]
        return o // 2, o % 2

    def local(i):
        unused, ox = owner(i)
        return lax.select(ox == x, vec_ref[my_rows(i), :], near[i // slots])

    def core_copy(d):
        return remote(core_out.at[d], core_in.at[d], cs_sem.at[d], cr_sem.at[d], core_dev)

    def y_copy(d):
        return remote(y_out.at[d], y_in.at[d], ys_sem.at[d], yr_sem.at[d], y_dev)

    rest_copy = remote(rest_out, rest_in, es_sem, er_sem, core_dev)

    for c in range(chunks):
        near_copy(c).start()

    lag_r = LAG * z
    lag_l = LAG * (last - z)
    lag_f = LAG * last
    first = lag_f + slots + 1

    def block(rows, count, cols):
        total = None
        for k in range(slots):
            term = jnp.dot(
                halves[:, k, rows, :].reshape(pairs * count, size), turned[k, :, cols],
                preferred_element_type=F32,
            )
            total = term if total is None else total + term
        return total.reshape(pairs, count, -1)

    def tile_at(yy, cc):
        return pl.ds(pl.multiple_of((yy * 2 + cc) * tile, 16), tile)

    def early_block(d):
        cols = block_at(d)
        core_out[d] = block(tile_at(1 - y, 1 - core), tile, cols).astype(BF16)
        core_copy(d).start()
        keep[d] = block(tile_at(1 - y, core), tile, cols)

    def early_send(d):
        core_copy(d).wait_recv()
        y_out[d] = (keep[d] + core_in[d].astype(F32)).astype(BF16)
        y_copy(d).start()

    others = pl.ds(pl.multiple_of((1 - y) * half, COLS), half)
    mine = pl.ds(pl.multiple_of(y * half, COLS), half)

    def half_of(c, p):
        rows = block_at(c)
        lhs = vectors[:, rows, :].reshape(slots * COLS, size)
        halves[p, :, rows, :] = (
            jnp.dot(lhs, amp[p], preferred_element_type=F32)
            .astype(BF16).reshape(slots, COLS, size)
        )

    def piece(c, r):
        @pl.when(r == 0)
        def _():
            for k in range(slots):
                final_copy(c * slots + k).wait_recv()
            for k in range(slots):
                turned[k, :, block_at(c)] = vectors[k, block_at(c), :].T
            half_of(c, 0)

        @pl.when(r == 1)
        def _():
            for p in range(1, pairs):
                half_of(c, p)

        @pl.when((r == 2) & (c == early - 1))
        def _():
            for d in range(early):
                early_block(d)

        @pl.when((r == 2) & (c >= early))
        def _():
            early_block(c)

        @pl.when((r == 3) & (c == early - 1))
        def _():
            for d in range(early):
                early_send(d)

        @pl.when((r == 3) & (c >= early))
        def _():
            at = pl.ds(pl.multiple_of((c - early) * COLS, 16), COLS)
            acc[:, at, others] = block(block_at(c), COLS, others)
            early_send(c)

    def step(t, carry):
        @pl.when((t < items) & (t % slots == 0))
        def _():
            near_copy(t // slots).wait_recv()

        i = t - lag_r

        @pl.when((i >= 0) & (i < items))
        def _():
            @pl.when(z > 0)
            def _():
                right_copy(i).wait_recv()

            @pl.when(z == 0)
            def _():
                right_out[i] = local(i)
                right_copy(i).start()

            @pl.when((z > 0) & (z < last))
            def _():
                oz, unused = owner(i)
                right_out[i] = lax.select(oz == z, local(i), right_in[i])
                right_copy(i).start()

        j = t - lag_l

        @pl.when((j >= 0) & (j < items))
        def _():
            @pl.when(z < last)
            def _():
                left_copy(j).wait_recv()

            @pl.when(z == last)
            def _():
                left_out[j] = local(j)
                left_copy(j).start()

            @pl.when((z > 0) & (z < last))
            def _():
                oz, unused = owner(j)
                left_out[j] = lax.select(oz == z, local(j), left_in[j])
                left_copy(j).start()

        f = t - lag_f

        @pl.when((f >= 0) & (f < items))
        def _():
            oz, unused = owner(f)
            k, rows = f % slots, my_rows(f)

            @pl.when(z == 0)
            def _():
                vectors[k, rows, :] = lax.select(oz == z, local(f), left_in[f])

            @pl.when(z == last)
            def _():
                vectors[k, rows, :] = lax.select(oz == z, local(f), right_in[f])

            @pl.when((z > 0) & (z < last))
            def _():
                came = lax.select(oz < z, right_in[f], left_in[f])
                vectors[k, rows, :] = lax.select(oz == z, local(f), came)

            final_copy(f).start()

        @pl.when(t == first)
        def _():
            load.wait()

        @pl.when(t >= first)
        def _():
            piece((t - first) // 4, (t - first) % 4)

        return carry

    lax.fori_loop(0, first + chunks * 4, step, 0)

    def sub(cc):
        return pl.ds(pl.multiple_of(cc * tile, 16), tile)

    rest_out[:, :, mine] = block(tile_at(y, 1 - core), tile, mine).astype(BF16)
    rest_out[:, :, others] = acc[:, sub(1 - core), others].astype(BF16)
    rest_copy.start()
    acc[:, sub(core), mine] = block(tile_at(y, core), tile, mine)
    rest_copy.wait_recv()
    for d in range(chunks):
        cols = block_at((d + early) % chunks)
        y_copy(d).wait_recv()
        out_ref[:, :, cols] = (
            acc[:, sub(core), cols] + rest_in[:, :, cols].astype(F32) + y_in[d].astype(F32)
        )

    for c in range(chunks):
        near_copy(c).wait_send()
        core_copy(c).wait_send()
        y_copy(c).wait_send()
    rest_copy.wait_send()

    def drain(i, carry):
        @pl.when(z < last)
        def _():
            right_copy(i).wait_send()

        @pl.when(z > 0)
        def _():
            left_copy(i).wait_send()

        final_copy(i).wait_send()
        return carry

    lax.fori_loop(0, items, drain, 0)


def on_device(pair_size, amplitudes, cholesky_vectors, owner_order):
    pairs, size, unused = amplitudes.shape
    slots = owner_order.shape[1]
    part = COLS // 2
    chunks = size // COLS
    items = slots * chunks
    tile = size // 4
    dma = pltpu.SemaphoreType.DMA
    vmem = pltpu.VMEM
    return pl.pallas_call(
        functools.partial(kernel, pair_size // 2, slots),
        out_shape=jax.ShapeDtypeStruct((pairs, tile, size), F32),
        in_specs=[
            pl.BlockSpec(memory_space=pltpu.SMEM),
            pl.BlockSpec(memory_space=pl.ANY),
            pl.BlockSpec(memory_space=pltpu.VMEM),
        ],
        out_specs=pl.BlockSpec(memory_space=pltpu.VMEM),
        scratch_shapes=[
            vmem((pairs, size, size), BF16),
            vmem((chunks, part, size), BF16),
            vmem((items, part, size), BF16),
            vmem((items, part, size), BF16),
            vmem((items, part, size), BF16),
            vmem((items, part, size), BF16),
            vmem((slots, size, size), BF16),
            vmem((slots, size, size), BF16),
            vmem((pairs, slots, size, size), BF16),
            vmem((pairs, size // 2, size), F32),
            vmem((chunks, pairs, tile, COLS), BF16),
            vmem((chunks, pairs, tile, COLS), BF16),
            vmem((chunks, pairs, tile, COLS), F32),
            vmem((chunks, pairs, tile, COLS), BF16),
            vmem((chunks, pairs, tile, COLS), BF16),
            vmem((pairs, tile, size), BF16),
            vmem((pairs, tile, size), BF16),
            dma,
            dma((chunks,)), dma((chunks,)),
            dma((items,)), dma((items,)),
            dma((items,)), dma((items,)),
            dma((items,)), dma((items,)),
            dma((chunks,)), dma((chunks,)),
            dma((chunks,)), dma((chunks,)),
            dma, dma,
        ],
        compiler_params=pltpu.CompilerParams(
            collective_id=0, has_side_effects=True, vmem_limit_bytes=58 * 2 ** 20
        ),
        cost_estimate=pl.CostEstimate(
            flops=4 * pairs * slots * size ** 3, bytes_accessed=8 * pairs * size ** 2,
            transcendentals=0,
        ),
    )(owner_order, amplitudes, cholesky_vectors[0, 0])


def solution(mesh):
    placed = (P("pair", None, None), P("vgrp", "pair", None, None), P())
    return jax.shard_map(
        functools.partial(on_device, mesh.shape["pair"]), mesh=mesh, in_specs=placed,
        out_specs=P("pair", "vgrp", None), check_vma=False,
    )
```

time: 104 us -> 95.4 us (0.917)
  Pallas kernels: 102 us -> 92.9 us
    pallas_call x1, Pallas kernels: 102 us -> 92.9 us  [on_device(): pl.pallas_call(functools.partial(kernel, pair_size // 2, slots), out_shap...]
    unnamed x3 -> x1, local copies, waits for them, and re-layouts: 1.7 us -> 2.36 us
where the time goes in v2:
time: 95.4 us; the launch traced here: 95.3 us
  Pallas kernels  92.9 us (97%)
  local copies, waits for them, and re-layouts  2.36 us (2%)
    pallas_call x1, Pallas kernels, on_device(): pl.pallas_call(functools.partial(kernel, pair_size // 2, slots), out_shap...  92.9 us
    unnamed x1, local copies, waits for them, and re-layouts  2.36 us

profile of v2, /device:TPU:0, one launch (start us, length us, event | category | flops | bytes accessed | tf_op | source)
XLA Modules:
  0.0 95.3 jit_solution(13479666526666757613)
XLA Ops:
  0.0 92.9 %shard_map.37 = f32[2,192,768]{2,1,0:T(8,128)} custom-call(s32[4,4]{1,0:T(4,128)} %owner_ref.1, bf16[2,768,768]{2,1,0:T(8,128)(2,1)} %amp_hbm.1, bf16[768,768]{1,0:T(8,128)(2,1)} %bitcast.1), custom_call_target="tpu_custom_call" | custom-call | flops 14495514624 | bytes 9437184 | tf_op jit(solution)/shard_map/pallas_call | solution.py:300
  92.9 2.4 %copy.5 = f32[2,192,768]{2,1,0:T(8,128)} copy(f32[2,192,768]{2,1,0:T(8,128)} %shard_map.37) | data formatting | bytes 2359296

commit v3 on v2

--- a/solution.py
+++ b/solution.py
@@ -9,7 +9,8 @@
 
 MESH = pl.DeviceIdType.MESH
 COLS = 128
-LAG = 2
+SPLIT = 2
+LAG = 3
 F32 = jnp.float32
 BF16 = jnp.bfloat16
 
@@ -27,10 +28,11 @@
     y, core = grp // 2, grp % 2
     size = vec_ref.shape[0]
     half = size // 2
-    part = COLS // 2
+    part = COLS // 2 // SPLIT
     chunks = size // COLS
     early = chunks // 2
-    items = slots * chunks
+    steps = slots * SPLIT
+    items = steps * chunks
     pairs, tile = out_ref.shape[0], out_ref.shape[1]
     last = nz - 1
 
@@ -58,8 +60,9 @@
         there = (c // early) * y + (1 - c // early) * (1 - y)
         return there * half + (c % early) * COLS
 
-    def rows_at(c, xx):
-        return pl.ds(pl.multiple_of(start_of(c) + xx * part, 16), part)
+    def rows_at(n, xx):
+        at = start_of(n // SPLIT) + (xx * SPLIT + n % SPLIT) * part
+        return pl.ds(pl.multiple_of(at, 16), part)
 
     def block_at(c):
         return pl.ds(pl.multiple_of(start_of(c), COLS), COLS)
@@ -98,13 +101,13 @@
 
     rest_copy = remote(rest_out, rest_in, es_sem, er_sem, core_dev)
 
-    for c in range(chunks):
+    for c in range(chunks * SPLIT):
         near_copy(c).start()
 
     lag_r = LAG * z
     lag_l = LAG * (last - z)
     lag_f = LAG * last
-    first = lag_f + slots + 1
+    first = lag_f + steps + 1
 
     def block(rows, count, cols):
         total = None
@@ -133,46 +136,62 @@
     others = pl.ds(pl.multiple_of((1 - y) * half, COLS), half)
     mine = pl.ds(pl.multiple_of(y * half, COLS), half)
 
-    def half_of(c, p):
+    def half_of(c, p, k0):
         rows = block_at(c)
-        lhs = vectors[:, rows, :].reshape(slots * COLS, size)
-        halves[p, :, rows, :] = (
+        count = slots // 2
+        lhs = vectors[pl.ds(k0, count), rows, :].reshape(count * COLS, size)
+        halves[p, pl.ds(k0, count), rows, :] = (
             jnp.dot(lhs, amp[p], preferred_element_type=F32)
-            .astype(BF16).reshape(slots, COLS, size)
+            .astype(BF16).reshape(count, COLS, size)
         )
+
+    def late_block(c):
+        at = pl.ds(pl.multiple_of((c - early) * COLS, 16), COLS)
+        acc[:, at, others] = block(block_at(c), COLS, others)
 
     def piece(c, r):
         @pl.when(r == 0)
         def _():
-            for k in range(slots):
-                final_copy(c * slots + k).wait_recv()
+            for n in range(steps):
+                final_copy(c * steps + n).wait_recv()
             for k in range(slots):
                 turned[k, :, block_at(c)] = vectors[k, block_at(c), :].T
-            half_of(c, 0)
-
-        @pl.when(r == 1)
-        def _():
-            for p in range(1, pairs):
-                half_of(c, p)
-
-        @pl.when((r == 2) & (c == early - 1))
-        def _():
-            for d in range(early):
+
+        for n in range(2 * pairs):
+            @pl.when(r == 1 + n)
+            def _(n=n):
+                half_of(c, n // 2, (n % 2) * (slots // 2))
+
+        at = 2 * pairs
+
+        for e in (early - 1, early):
+            d = (e - early + 1) * 2
+
+            @pl.when((c == e) & (r == at + 1))
+            def _(d=d):
                 early_block(d)
 
-        @pl.when((r == 2) & (c >= early))
+            @pl.when((c == e) & (r == at + 2))
+            def _(d=d):
+                early_block(d + 1)
+
+            @pl.when((c == e) & (r == at + 3))
+            def _(d=d, e=e):
+                if e == early:
+                    late_block(e)
+                early_send(d)
+                early_send(d + 1)
+
+        @pl.when((c > early) & (r == at + 1))
         def _():
             early_block(c)
 
-        @pl.when((r == 3) & (c == early - 1))
-        def _():
-            for d in range(early):
-                early_send(d)
-
-        @pl.when((r == 3) & (c >= early))
-        def _():
-            at = pl.ds(pl.multiple_of((c - early) * COLS, 16), COLS)
-            acc[:, at, others] = block(block_at(c), COLS, others)
+        @pl.when((c > early) & (r == at + 2))
+        def _():
+            late_block(c)
+
+        @pl.when((c > early) & (r == at + 3))
+        def _():
             early_send(c)
 
     def step(t, carry):
@@ -246,11 +265,11 @@
 
         @pl.when(t >= first)
         def _():
-            piece((t - first) // 4, (t - first) % 4)
+            piece((t - first) // steps, (t - first) % steps)
 
         return carry
 
-    lax.fori_loop(0, first + chunks * 4, step, 0)
+    lax.fori_loop(0, first + chunks * steps, step, 0)
 
     def sub(cc):
         return pl.ds(pl.multiple_of(cc * tile, 16), tile)
@@ -267,8 +286,9 @@
             acc[:, sub(core), cols] + rest_in[:, :, cols].astype(F32) + y_in[d].astype(F32)
         )
 
+    for c in range(chunks * SPLIT):
+        near_copy(c).wait_send()
     for c in range(chunks):
-        near_copy(c).wait_send()
         core_copy(c).wait_send()
         y_copy(c).wait_send()
     rest_copy.wait_send()
@@ -291,9 +311,9 @@
 def on_device(pair_size, amplitudes, cholesky_vectors, owner_order):
     pairs, size, unused = amplitudes.shape
     slots = owner_order.shape[1]
-    part = COLS // 2
+    part = COLS // 2 // SPLIT
     chunks = size // COLS
-    items = slots * chunks
+    items = slots * chunks * SPLIT
     tile = size // 4
     dma = pltpu.SemaphoreType.DMA
     vmem = pltpu.VMEM
@@ -308,7 +328,7 @@
         out_specs=pl.BlockSpec(memory_space=pltpu.VMEM),
         scratch_shapes=[
             vmem((pairs, size, size), BF16),
-            vmem((chunks, part, size), BF16),
+            vmem((chunks * SPLIT, part, size), BF16),
             vmem((items, part, size), BF16),
             vmem((items, part, size), BF16),
             vmem((items, part, size), BF16),
@@ -325,7 +345,7 @@
             vmem((pairs, tile, size), BF16),
             vmem((pairs, tile, size), BF16),
             dma,
-            dma((chunks,)), dma((chunks,)),
+            dma((chunks * SPLIT,)), dma((chunks * SPLIT,)),
             dma((items,)), dma((items,)),
             dma((items,)), dma((items,)),
             dma((items,)), dma((items,)),

time: 95.4 us -> 105 us (1.10)
  Pallas kernels: 92.9 us -> 103 us
    pallas_call x1, Pallas kernels: 92.9 us -> 103 us  [on_device(): pl.pallas_call(functools.partial(kernel, pair_size // 2, slots), out_shap...]
where the time goes in v3:
time: 105 us
  Pallas kernels  103 us (98%)
  local copies, waits for them, and re-layouts  2.36 us (2%)
    pallas_call x1, Pallas kernels, on_device(): pl.pallas_call(functools.partial(kernel, pair_size // 2, slots), out_shap...  103 us
    unnamed x1, local copies, waits for them, and re-layouts  2.36 us

profile of v3, /device:TPU:0, one launch (start us, length us, event | category | flops | bytes accessed | tf_op | source)
XLA Modules:
  0.0 104.9 jit_solution(5995729567282400307)
XLA Ops:
  0.0 102.5 %shard_map.37 = f32[2,192,768]{2,1,0:T(8,128)} custom-call(s32[4,4]{1,0:T(4,128)} %owner_ref.1, bf16[2,768,768]{2,1,0:T(8,128)(2,1)} %amp_hbm.1, bf16[768,768]{1,0:T(8,128)(2,1)} %bitcast.1), custom_call_target="tpu_custom_call" | custom-call | flops 14495514624 | bytes 9437184 | tf_op jit(solution)/shard_map/pallas_call | solution.py:320
  102.5 2.4 %copy.5 = f32[2,192,768]{2,1,0:T(8,128)} copy(f32[2,192,768]{2,1,0:T(8,128)} %shard_map.37) | data formatting | bytes 2359296
